TPU v7x, 256 devices: a whole 4x4x8 slice. The times are simulated.
256 devices in a mesh: row: 8 (over z_lo, core), col: 32 (over z_hi, x, y).
Axes of the slice: x: 4, y: 4, z: 8 (z_hi: 2, z_lo: 4; z = z_hi * 4 + z_lo), core: 2. Of those that a mesh axis runs over, the one named last changes fastest.
Arguments:
- object_field: float32 [2, 2048, 8192], P(None, 'row', 'col'), may hold values from -6 to 6
- probe: float32 [4, 2, 128, 128], replicated, may hold values from -4 to 4
- offsets: int32 [2048, 2], P(('row', 'col')), may hold values from 0 to 255, as said below
- counts: int32 [256], P(('row', 'col')), may hold values from 4 to 8, as said below
- amplitudes: float32 [2048, 128, 128], P(('row', 'col')), may hold values from 0.1 to 3
Outputs:
- new_object: float32 [2, 2048, 8192], P(None, 'row', 'col')
- probe_direction: float32 [4, 2, 128, 128], replicated
Inputs may be any that keep to these rules, and one draw needn't show every extreme that they name: Every pattern window lies inside the object: in the last tile row offsets[g,0] <= 128, in the last tile column offsets[g,1] <= 128; elsewhere a window may reach into the tiles below and to the right. Offsets are below their tile's side. `counts`: some tile has all 8 slots live.
All inputs are finite; a program needn't handle non-finite values.
Results may differ from a plain program's by a relative error of at most 0.0003.
Values sent between devices are 32-bit elements; how exact they have to be, the bound alone decides.
A program may use at most 128 MiB of HBM per device.

v0:
```python
import functools

import jax
import jax.numpy as jnp
import ml_dtypes
import numpy as np
from jax import lax
from jax.experimental import pallas as pl
from jax.experimental.pallas import tpu as pltpu
from jax.sharding import PartitionSpec as P

BF = jnp.bfloat16
F32 = jnp.float32
W = 128
MESH = pl.DeviceIdType.MESH
HBM = pl.BlockSpec(memory_space=pl.ANY)
VMEM = pl.BlockSpec(memory_space=pltpu.VMEM)
SMEM = pl.BlockSpec(memory_space=pltpu.SMEM)
LIMIT = 56 * 2**20


def tables():
    index = np.arange(W)
    angle = (index[:, None] * index[None, :] % W) * (2 * np.pi / W)
    cosine, sine = np.cos(angle) / np.sqrt(W), np.sin(angle) / np.sqrt(W)

    def split(matrix):
        matrix = matrix.astype(np.float32)
        high = matrix.astype(ml_dtypes.bfloat16)
        return high, (matrix - high.astype(np.float32)).astype(ml_dtypes.bfloat16)

    fwd = split(np.block([[cosine, -sine], [sine, cosine]]))
    inv = split(np.block([[cosine, sine], [-sine, cosine]]))
    return fwd, inv


def position():
    return lax.axis_index("row"), lax.axis_index("col")


def count(*flags):
    return sum(flag.astype(jnp.int32) for flag in flags)


PLANE = 16
HALO_RELAYS = (12, 4, 1, 3, 15, 5, 13, 7)
SUMS_RELAYS = (0, 12, 13, 14)


def hilo(x):
    high = x.astype(BF)
    return high, (x - high.astype(F32)).astype(BF)


def dot(a, b):
    return jnp.dot(a, b, preferred_element_type=F32)


def columns(parts):
    return jnp.concatenate(parts, axis=1)


def rows_of(parts):
    return jnp.concatenate(parts, axis=0)


def times_right(high, low, table):
    out = dot(columns([high, low, high]), table[...])
    return [(out[k * W : (k + 1) * W, :W], out[k * W : (k + 1) * W, W:]) for k in range(2)]


def times_left(pairs, table):
    high, low = hilo(columns([rows_of(pair) for pair in pairs]))
    out = dot(table[...], high)
    out = out[: 2 * W] + out[2 * W :] + dot(table[: 2 * W], low)
    return [(out[:W, k * W : (k + 1) * W], out[W:, k * W : (k + 1) * W]) for k in range(2)]


def forward(s, place, ext, probe, amps, table_right, table_left, patch, psi, far_high, far_low, sums):
    top, left, live = place
    block, lanes = left // W, left % W
    lane = lax.broadcasted_iota(jnp.int32, (W, W), 1)
    kept = lane < live * W

    def cut(plane):
        first = ext[plane, block, pl.ds(top, W), :]
        second = ext[plane, block + 1, pl.ds(top, W), :]
        turned = pltpu.roll(jnp.where(lane >= lanes, first, second), (W - lanes) % W, 1)
        return jnp.where(kept, turned, 0.0)

    ore, oim = cut(0), cut(1)
    patch[s, 0], patch[s, 1] = ore, oim
    add_plane(sums, 8, ore * ore + oim * oim)
    inten = jnp.zeros((W, W), F32)
    far = []
    for g in range(0, probe.shape[0], 2):
        for m in (g, g + 1):
            psi[s, m, 0] = probe[m, 0] * ore - probe[m, 1] * oim
            psi[s, m, 1] = probe[m, 0] * oim + probe[m, 1] * ore
        high, low = hilo(rows_of([columns([psi[s, m, 0], psi[s, m, 1]]) for m in (g, g + 1)]))
        pairs = times_left(times_right(high, low, table_right), table_left)
        for real, imag in pairs:
            inten = inten + (real * real + imag * imag)
        far += pairs
    factor = amps[s] * lax.rsqrt(jnp.maximum(inten, 0.25))
    for m, (real, imag) in enumerate(far):
        far_high[s, m], far_low[s, m] = hilo(columns([real * factor, imag * factor]))


def backward(s, probe, table_right, table_left, patch, psi, far_high, far_low, sums):
    num_re, num_im = jnp.zeros((W, W), F32), jnp.zeros((W, W), F32)
    for g in range(0, probe.shape[0], 2):
        high, low = rows_of([far_high[s, g], far_high[s, g + 1]]), rows_of([far_low[s, g], far_low[s, g + 1]])
        pairs = times_left(times_right(high, low, table_right), table_left)
        for m, (real, imag) in zip((g, g + 1), pairs):
            chi_re, chi_im = real - psi[s, m, 0], imag - psi[s, m, 1]
            num_re = num_re + (probe[m, 0] * chi_re + probe[m, 1] * chi_im)
            num_im = num_im + (probe[m, 0] * chi_im - probe[m, 1] * chi_re)
            add_plane(sums, 2 * m, patch[s, 0] * chi_re + patch[s, 1] * chi_im)
            add_plane(sums, 2 * m + 1, patch[s, 0] * chi_im - patch[s, 1] * chi_re)
    return num_re, num_im


DEPTH = 8
UNIT = W // 8
TILES = 10 * UNIT
HALF = TILES // 2
SHARE = HALF // PLANE


def add_plane(sums, plane, value):
    here = pl.ds(plane * UNIT, UNIT)
    sums[here] += value.reshape(UNIT, 8, W)


def placed(shifted, plane, place, count, acc, target):
    lane = lax.broadcasted_iota(jnp.int32, (W, W), 1)
    for part in range(3):

        def add(s, blocks):
            top, left, live = place(s)
            value = shifted[s, plane, pl.ds(2 * W + part * W - top, W), :]
            out = []
            for j, block in enumerate(blocks):
                at = lane + (j * W - left)
                inside = jnp.logical_and(at >= 0, at < live * W)
                out.append(block + jnp.where(inside, value, 0.0))
            return tuple(out)

        blocks = lax.fori_loop(0, count, add, tuple(jnp.zeros((W, W), F32) for _ in range(3)), unroll=True)
        for j in range(3):
            acc[target, j, pl.ds(part * W, W), :] = blocks[j]


def step_kernel(rows, cols, offsets_hbm, counts_hbm, *refs):
    (obj, *hbm), (updated, direction) = refs[:7], refs[7:9]
    (offsets, counts, patch, psi, far_high, far_low, shifted, acc, sums, got, gathered, shard, layers, total) = refs[9:23]
    (from_left, from_above, from_corner, from_high, relay, halo_relay) = refs[23:29]
    (load, halo_send, halo_recv, send, recv, ar_send, ar_recv, ext, *vmem) = refs[29:]
    probe, amps, right_fwd, right_inv, left_fwd, left_inv = vmem
    slot_count = amps.shape[0]
    r, c = position()
    core, z_lo = lax.rem(r, 2), r // 2
    z_hi, xy = c // PLANE, lax.rem(c, PLANE)
    z = z_hi * (DEPTH // 2) + z_lo
    left, up = c > 0, r > 0
    right, down = c < cols - 1, r < rows - 1
    up_left, down_right = jnp.logical_and(up, left), jnp.logical_and(down, right)
    near_right, near_left = jnp.logical_and(right, c != PLANE - 1), jnp.logical_and(left, c != PLANE)
    up_right, turning = jnp.logical_and(up, near_right), jnp.logical_and(down, near_right)
    source, target = c == PLANE - 1, c == PLANE
    target_up = jnp.logical_and(target, up)
    passing = [c == spot for spot in SUMS_RELAYS]
    passing = passing[:2] + [jnp.logical_and(flag, down) for flag in passing[2:]]
    sourced = [source] * 2 + [jnp.logical_and(source, down)] * 2
    east, south, southeast = (r, c + 1), (r + 1, c), (r + 1, c + 1)
    twin = (r + 1 - 2 * core, c)

    def in_plane(k):
        other = lax.rem(xy + k, PLANE)
        return other, (r, z_hi * PLANE + other)

    def in_depth(k):
        other = lax.rem(z + k, DEPTH)
        half = DEPTH // 2
        return lax.rem(other, half) * 2 + core, (other // half) * PLANE + xy

    pieces = [(obj.at[:, :, pl.ds(k * W, W)], ext.at[:, k, pl.ds(0, 2 * W)]) for k in range(2)]
    pieces += [(offsets_hbm, offsets), (counts_hbm, counts)]
    pieces += list(zip(hbm, vmem))
    copies = [pltpu.make_async_copy(src, dst, load.at[k]) for k, (src, dst) in enumerate(pieces)]
    for copy in copies:
        copy.start()

    barrier = pltpu.get_barrier_semaphore()
    peers = [twin] + [in_plane(k)[1] for k in range(1, PLANE)] + [in_depth(k) for k in range(1, DEPTH)]
    ahead = [c == PLANE + spot for spot in HALO_RELAYS]
    ahead_up = [jnp.logical_and(flag, up) for flag in ahead]
    target_down = jnp.logical_and(source, down)
    greetings = [(source, (r, PLANE + spot)) for spot in HALO_RELAYS]
    greetings += [(target_down, (r + 1, PLANE + spot)) for spot in HALO_RELAYS]
    greetings += [(flag, (r, PLANE)) for flag in ahead] + [(near_right, east), (down, south)]
    waits = [near_left, up, *[target for _ in HALO_RELAYS], *ahead, *ahead_up]
    greetings += [(left, (r, c - 1)), (up, (r - 1, c)), (up_left, (r - 1, c - 1))]
    greetings += [(target, (r, spot)) for spot in SUMS_RELAYS[:2]]
    greetings += [(target_up, (r - 1, spot)) for spot in SUMS_RELAYS[2:]]
    greetings += [(flag, (r, PLANE - 1)) for flag in passing]
    for when, device in greetings:

        @pl.when(when)
        def _():
            pl.semaphore_signal(barrier, inc=1, device_id=device, device_id_type=MESH)

    for device in peers:
        pl.semaphore_signal(barrier, inc=1, device_id=device, device_id_type=MESH)
    waits += [right, down, down_right, *sourced, *passing]

    def place(s):
        return offsets[0, s], offsets[1, s], (s < counts[0, 0]).astype(jnp.int32)

    def remote(k, src, dst, device):
        return pltpu.make_async_remote_copy(src, dst, send.at[k], recv.at[k], device_id=device, device_id_type=MESH)

    def summed(k, src, dst, device):
        return pltpu.make_async_remote_copy(src, dst, ar_send.at[k], ar_recv.at[k], device_id=device, device_id_type=MESH)

    def halo(k, src, dst, device):
        return pltpu.make_async_remote_copy(
            src, dst, halo_send.at[k], halo_recv.at[k], device_id=device, device_id_type=MESH
        )

    upper, lower, under_rows = pl.ds(0, W), pl.ds(W, W), pl.ds(2 * W, W)
    west, north = (r, c - 1), (r - 1, c)
    exchange = [
        (near_left, near_right, halo(0, ext.at[:, 0, upper], ext.at[:, 2, upper], west)),
        (up, down, halo(1, ext.at[:, 0, upper], ext.at[:, 0, under_rows], north)),
        (up, down, halo(2, ext.at[:, 1, upper], ext.at[:, 1, under_rows], north)),
        (near_left, near_right, halo(3, ext.at[:, 0, lower], ext.at[:, 2, lower], west)),
    ]
    handed = halo(4, ext.at[:, 2, upper], ext.at[:, 2, under_rows], north)
    relays = len(HALO_RELAYS)
    share = 2 * W // relays
    there, back, above = [], [], []
    for half in range(2):
        for i, spot in enumerate(HALO_RELAYS):
            plane, start = i % 2, i // 2 * share
            span, k = pl.ds(half * W + start, share), 5 + half * relays + i
            held = halo_relay.at[half]
            there.append((target, ahead[i], halo(k, ext.at[plane, 0, span], held, (r, PLANE + spot))))
            back.append((ahead[i], source, halo(k + 2 * relays, held, ext.at[plane, 2, span], (r, PLANE - 1))))
            if half == 0:
                corner_rows = ext.at[plane, 2, pl.ds(2 * W + start, share)]
                above.append((ahead_up[i], target_down, halo(k + 4 * relays, held, corner_rows, (r - 1, PLANE - 1))))
    for copy in copies[:2]:
        copy.wait()
    pl.semaphore_wait(barrier, len(peers) + count(*waits))
    for sends, _, copy in there + exchange:
        pl.when(sends)(copy.start)

    shifted[...] = jnp.zeros_like(shifted)
    sums[...] = jnp.zeros_like(sums)
    for copy in copies[2:]:
        copy.wait()

    power = jnp.zeros((W, W), F32)
    for m in range(probe.shape[0]):
        power = power + (probe[m, 0] * probe[m, 0] + probe[m, 1] * probe[m, 1])

    def weigh(s, carry):
        shifted[s, 2, pl.ds(2 * W, W), :] = pltpu.roll(power, place(s)[1] % W, 1)
        return carry

    lax.fori_loop(0, slot_count, weigh, 0, unroll=True)
    placed(shifted, 2, place, slot_count, acc, 2)
    strip, under, corner = acc.at[:, 2, pl.ds(0, 2 * W)], acc.at[:, pl.ds(0, 2), pl.ds(2 * W, W)], acc.at[:, 2, pl.ds(2 * W, W)]
    weights = [
        (right, left, remote(0, strip.at[2], from_left.at[2], east)),
        (down, up, remote(1, under.at[2], from_above.at[2], south)),
        (down_right, up_left, remote(2, corner.at[2], from_corner.at[2], southeast)),
    ]
    for sends, _, copy in weights:
        pl.when(sends)(copy.start)

    for (_, flag, arriving), (_, _, leaving) in zip(there, back):

        @pl.when(flag)
        def _():
            arriving.wait_recv()
            leaving.start()

    for flag, _, copy in above:
        pl.when(flag)(copy.start)
    pl.when(near_right)(exchange[0][2].wait_recv)
    pl.when(up_right)(handed.start)
    for _, receives, copy in exchange[1:] + back + above + [(up_right, turning, handed)]:
        pl.when(receives)(copy.wait_recv)

    def first(s, carry):
        forward(s, place(s), ext, probe, amps, right_fwd, left_fwd, patch, psi, far_high, far_low, sums)
        return carry

    lax.fori_loop(0, slot_count, first, 0, unroll=True)

    def second(s, carry):
        turn = place(s)[1] % W
        for plane, value in enumerate(backward(s, probe, right_inv, left_inv, patch, psi, far_high, far_low, sums)):
            shifted[s, plane, pl.ds(2 * W, W), :] = pltpu.roll(value, turn, 1)
        return carry

    lax.fori_loop(0, slot_count, second, 0, unroll=True)

    mine = pl.ds(core * HALF, HALF)
    swap = summed(0, sums.at[pl.ds((1 - core) * HALF, HALF)], got, twin)
    swap.start()
    placed(shifted, 0, place, slot_count, acc, 0)
    swap.wait_recv()
    got[...] += sums[mine]

    scatter = []
    for k in range(1, PLANE):
        other, device = in_plane(k)
        scatter.append(summed(k, got.at[pl.ds(other * SHARE, SHARE)], gathered.at[k - 1], device))
        scatter[-1].start()
    placed(shifted, 1, place, slot_count, acc, 1)
    numer = pl.ds(0, 2)
    crossing = [(strip.at[p, lower], from_left.at[p, lower], (r, PLANE)) for p in range(2)]
    crossing += [(corner.at[p], from_corner.at[p], (r + 1, PLANE)) for p in range(2)]
    pass_on = [remote(3 + i, src, relay, (r, spot)) for i, ((src, _, _), spot) in enumerate(zip(crossing, SUMS_RELAYS))]
    passed = [remote(7 + i, relay, dst, device) for i, (_, dst, device) in enumerate(crossing)]
    turned = remote(11, corner.at[numer], from_high, south)
    plan = [
        (turning, up_right, turned),
        (near_right, near_left, remote(12, strip.at[numer, lower], from_left.at[numer, lower], east)),
        (down, up, remote(13, under.at[numer], from_above.at[numer], south)),
    ]
    late = remote(14, strip.at[numer, upper], from_left.at[numer, upper], east)
    for flag, copy in zip(sourced, pass_on):
        pl.when(flag)(copy.start)
    pl.when(source)(late.start)
    for sends, _, copy in plan:
        pl.when(sends)(copy.start)
    value = got[pl.ds(xy * SHARE, SHARE)]
    for k in range(1, PLANE):
        scatter[k - 1].wait_recv()
        value = value + gathered[k - 1]
    shard[...] = value

    spread = []
    for k in range(1, DEPTH):
        spread.append(summed(PLANE - 1 + k, shard, layers.at[z], in_depth(k)))
        spread[-1].start()
    layers[z] = value
    for flag, arriving, leaving in zip(passing, pass_on, passed):

        @pl.when(flag)
        def _():
            arriving.wait_recv()
            leaving.start()

    @pl.when(up_right)
    def _():
        turned.wait_recv()
        strip[numer, upper] += from_high[...]

    pl.when(near_right)(late.start)
    for copy in spread:
        copy.wait_recv()
    value = layers[0]
    for k in range(1, DEPTH):
        value = value + layers[k]
    here = pl.ds(core * HALF + xy * SHARE, SHARE)
    total[here] = value

    gather = []
    for k in range(1, PLANE):
        gather.append(summed(PLANE + DEPTH - 2 + k, total.at[here], total.at[here], in_plane(k)[1]))
        gather[-1].start()

    for copy in gather:
        copy.wait_recv()
    half = total.at[mine]
    last = summed(2 * PLANE + DEPTH - 2, half, half, twin)
    last.start()

    for _, receives, copy in weights + plan[1:]:
        pl.when(receives)(copy.wait_recv)
    for flag, copy in zip([target] * 2 + [target_up] * 2, passed):
        pl.when(flag)(copy.wait_recv)
    pl.when(left)(late.wait_recv)

    def taken(flag, value):
        return jnp.where(jnp.broadcast_to(flag.astype(jnp.int32), value.shape) > 0, value, 0.0)

    for i in range(2):
        for j in range(2):
            span = pl.ds(i * W, W)
            parts = []
            for plane in range(3):
                value = acc[plane, j, span, :]
                if j == 0:
                    value = value + taken(left, from_left[plane, span, :])
                if i == 0:
                    value = value + taken(up, from_above[plane, j])
                if i == 0 and j == 0:
                    value = value + taken(up_left if plane == 2 else target_up, from_corner[plane])
                parts.append(value)
            scale = 1.0 / (parts[2] + 1.0)
            for plane in range(2):
                updated[plane, span, pl.ds(j * W, W)] = ext[plane, j, span, :] + parts[plane] * scale

    last.wait_recv()
    scale = lax.rsqrt(total[pl.ds(8 * UNIT, UNIT)] + 1.0)
    for plane in range(8):
        direction[plane] = total[pl.ds(plane * UNIT, UNIT)] * scale
    for copy in [swap, *scatter, *spread, *gather, last]:
        copy.wait_send()
    for sends, _, copy in exchange + there + back + above + [(up_right, turning, handed)] + weights + plan:
        pl.when(sends)(copy.wait_send)
    for flag, copy in zip(sourced + passing, pass_on + passed):
        pl.when(flag)(copy.wait_send)
    pl.when(right)(late.wait_send)


def step(obj, probe, offsets, counts, amps, rows, cols):
    fwd, inv = tables()
    consts = [
        np.concatenate([fwd[0], fwd[0], fwd[1]], 0),
        np.concatenate([inv[0], inv[0], inv[1]], 0),
        np.concatenate([inv[0], inv[1]], 0),
        np.concatenate([fwd[0], fwd[1]], 0),
    ]
    loaded = [probe, amps] + [jnp.asarray(v) for v in consts]
    slot_count, modes = amps.shape[0], probe.shape[0]
    dma = pltpu.SemaphoreType.DMA
    messages = 2 * PLANE + DEPTH - 1
    return pl.pallas_call(
        functools.partial(step_kernel, rows, cols),
        out_shape=(
            pltpu.VMEM(obj.shape, F32),
            pltpu.VMEM((8, UNIT, 8, W), F32),
        ),
        in_specs=[HBM] * 9,
        out_specs=(VMEM, VMEM),
        scratch_shapes=[
            pltpu.SMEM(offsets.shape[::-1], jnp.int32),
            pltpu.SMEM((1, 1), jnp.int32),
            pltpu.VMEM((slot_count, 2, W, W), F32),
            pltpu.VMEM((slot_count, modes, 2, W, W), F32),
            pltpu.VMEM((slot_count, modes, W, 2 * W), BF),
            pltpu.VMEM((slot_count, modes, W, 2 * W), BF),
            pltpu.VMEM((slot_count, 3, 5 * W, W), F32),
            pltpu.VMEM((3, 3, 3 * W, W), F32),
            pltpu.VMEM((TILES, 8, W), F32),
            pltpu.VMEM((HALF, 8, W), F32),
            pltpu.VMEM((PLANE - 1, SHARE, 8, W), F32),
            pltpu.VMEM((SHARE, 8, W), F32),
            pltpu.VMEM((DEPTH, SHARE, 8, W), F32),
            pltpu.VMEM((TILES, 8, W), F32),
            pltpu.VMEM((3, 2 * W, W), F32),
            pltpu.VMEM((3, 2, W, W), F32),
            pltpu.VMEM((3, W, W), F32),
            pltpu.VMEM((2, W, W), F32),
            pltpu.VMEM((W, W), F32),
            pltpu.VMEM((2, 2 * W // len(HALO_RELAYS), W), F32),
            dma((10,)),
            dma((5 + 5 * len(HALO_RELAYS),)),
            dma((5 + 5 * len(HALO_RELAYS),)),
            dma((15,)),
            dma((15,)),
            dma((messages,)),
            dma((messages,)),
            pltpu.VMEM((2, 3, 3 * W, W), F32),
        ]
        + [pltpu.VMEM(v.shape, v.dtype) for v in loaded],
        compiler_params=pltpu.CompilerParams(collective_id=0, has_side_effects=True, vmem_limit_bytes=LIMIT),
        name="step",
    )(offsets.T, counts[None], obj, *loaded)


def body(rows, cols, object_field, probe, offsets, counts, amplitudes):
    new_object, direction = step(object_field, probe, offsets, counts, amplitudes, rows, cols)
    return new_object, direction.reshape(probe.shape)


def solution(mesh):
    rows, cols = mesh.shape["row"], mesh.shape["col"]
    return jax.shard_map(
        functools.partial(body, rows, cols),
        mesh=mesh,
        in_specs=(
            P(None, "row", "col"),
            P(),
            P(("row", "col"), None),
            P(("row", "col")),
            P(("row", "col"), None, None),
        ),
        out_specs=(P(None, "row", "col"), P()),
        check_vma=False,
    )
```

profile of v0, /device:TPU:1, one launch (start us, length us, event | category | flops | bytes accessed | tf_op | source)
XLA Modules:
  0.0 59.3 jit_solution(3274689467072664827)
XLA Ops:
  1.3 56.4 %step.1 = (f32[2,256,256]{2,1,0:T(8,128)S(1)}, f32[8,16,8,128]{3,2,1,0:T(8,128)S(1)}) custom-call(s32[2,8]{1,0:T(2,128)} %bitcast.5, s32[1,1]{1,0:T(1,128)} %bitcast.3.counts_hbm, f32[2,256,256]{2,1,0:T(8,128)} %refs_0_.1, f32[4,2,128,128]{3,2,1,0:T(8,128)} %refs_1_.1, f32[8,128,128]{2,1,0:T(8,128)} %refs_2_.1, bf16[768,256]{1,0:T(8,128)(2,1)} %constant.8.clone.refs_3_, ...), custom_call_target="tpu_custom_call" | custom-call | tf_op jit(solution)/shard_map/step/pallas_call | solution.py:436
  57.7 0.8 %copy.13 = f32[2,256,256]{2,1,0:T(8,128)} copy(f32[2,256,256]{2,1,0:T(8,128)S(1)} %get-tuple-element.6) | data formatting | bytes 1048576
  58.5 0.8 %copy.14 = f32[4,2,128,128]{3,2,1,0:T(8,128)} copy(f32[4,2,128,128]{3,2,1,0:T(8,128)S(1)} %bitcast.4) | data formatting | bytes 1048576
where the time goes:
time: 59.4 us; the launch traced here: 59.3 us
  Pallas kernels  56.4 us (95%)
  local copies, waits for them, and re-layouts  1.59 us (3%)
  between operations  1.29 us (2%)
    pallas_call x1, Pallas kernels, step(): pl.pallas_call(functools.partial(step_kernel, rows, cols), out_shape=(plt...  56.4 us
    unnamed x2, local copies, waits for them, and re-layouts  1.59 us

commit v1 on v0

--- a/solution.py
+++ b/solution.py
@@ -218,39 +218,46 @@
     def place(s):
         return offsets[0, s], offsets[1, s], (s < counts[0, 0]).astype(jnp.int32)
 
-    def remote(k, src, dst, device):
-        return pltpu.make_async_remote_copy(src, dst, send.at[k], recv.at[k], device_id=device, device_id_type=MESH)
+    def remote(k, j, src, dst, device):
+        return pltpu.make_async_remote_copy(src, dst, send.at[k], recv.at[j], device_id=device, device_id_type=MESH)
+
+    def landed(when, ref, semaphore):
+        wait = pltpu.make_async_copy(ref, ref, semaphore).wait
+        if when is None:
+            wait()
+        else:
+            pl.when(when)(wait)
 
     def summed(k, src, dst, device):
         return pltpu.make_async_remote_copy(src, dst, ar_send.at[k], ar_recv.at[k], device_id=device, device_id_type=MESH)
 
-    def halo(k, src, dst, device):
+    def halo(k, j, src, dst, device):
         return pltpu.make_async_remote_copy(
-            src, dst, halo_send.at[k], halo_recv.at[k], device_id=device, device_id_type=MESH
+            src, dst, halo_send.at[k], halo_recv.at[j], device_id=device, device_id_type=MESH
         )
 
     upper, lower, under_rows = pl.ds(0, W), pl.ds(W, W), pl.ds(2 * W, W)
     west, north = (r, c - 1), (r - 1, c)
     exchange = [
-        (near_left, near_right, halo(0, ext.at[:, 0, upper], ext.at[:, 2, upper], west)),
-        (up, down, halo(1, ext.at[:, 0, upper], ext.at[:, 0, under_rows], north)),
-        (up, down, halo(2, ext.at[:, 1, upper], ext.at[:, 1, under_rows], north)),
-        (near_left, near_right, halo(3, ext.at[:, 0, lower], ext.at[:, 2, lower], west)),
+        (near_left, near_right, halo(0, 0, ext.at[:, 0, upper], ext.at[:, 2, upper], west)),
+        (up, down, halo(1, 1, ext.at[:, 0, upper], ext.at[:, 0, under_rows], north)),
+        (up, down, halo(2, 2, ext.at[:, 1, upper], ext.at[:, 1, under_rows], north)),
+        (near_left, near_right, halo(3, 3, ext.at[:, 0, lower], ext.at[:, 2, lower], west)),
     ]
-    handed = halo(4, ext.at[:, 2, upper], ext.at[:, 2, under_rows], north)
+    handed = halo(4, 4, ext.at[:, 2, upper], ext.at[:, 2, under_rows], north)
     relays = len(HALO_RELAYS)
     share = 2 * W // relays
     there, back, above = [], [], []
     for half in range(2):
         for i, spot in enumerate(HALO_RELAYS):
             plane, start = i % 2, i // 2 * share
-            span, k = pl.ds(half * W + start, share), 5 + half * relays + i
+            span = pl.ds(half * W + start, share)
             held = halo_relay.at[half]
-            there.append((target, ahead[i], halo(k, ext.at[plane, 0, span], held, (r, PLANE + spot))))
-            back.append((ahead[i], source, halo(k + 2 * relays, held, ext.at[plane, 2, span], (r, PLANE - 1))))
+            there.append((target, ahead[i], halo(5, 5 + half, ext.at[plane, 0, span], held, (r, PLANE + spot))))
+            back.append((ahead[i], source, halo(6 + half, 7 + half, held, ext.at[plane, 2, span], (r, PLANE - 1))))
             if half == 0:
                 corner_rows = ext.at[plane, 2, pl.ds(2 * W + start, share)]
-                above.append((ahead_up[i], target_down, halo(k + 4 * relays, held, corner_rows, (r - 1, PLANE - 1))))
+                above.append((ahead_up[i], target_down, halo(8, 9, held, corner_rows, (r - 1, PLANE - 1))))
     for copy in copies[:2]:
         copy.wait()
     pl.semaphore_wait(barrier, len(peers) + count(*waits))
@@ -274,9 +281,9 @@
     placed(shifted, 2, place, slot_count, acc, 2)
     strip, under, corner = acc.at[:, 2, pl.ds(0, 2 * W)], acc.at[:, pl.ds(0, 2), pl.ds(2 * W, W)], acc.at[:, 2, pl.ds(2 * W, W)]
     weights = [
-        (right, left, remote(0, strip.at[2], from_left.at[2], east)),
-        (down, up, remote(1, under.at[2], from_above.at[2], south)),
-        (down_right, up_left, remote(2, corner.at[2], from_corner.at[2], southeast)),
+        (right, left, remote(0, 0, strip.at[2], from_left.at[2], east)),
+        (down, up, remote(1, 1, under.at[2], from_above.at[2], south)),
+        (down_right, up_left, remote(2, 2, corner.at[2], from_corner.at[2], southeast)),
     ]
     for sends, _, copy in weights:
         pl.when(sends)(copy.start)
@@ -292,8 +299,11 @@
         pl.when(flag)(copy.start)
     pl.when(near_right)(exchange[0][2].wait_recv)
     pl.when(up_right)(handed.start)
-    for _, receives, copy in exchange[1:] + back + above + [(up_right, turning, handed)]:
+    for _, receives, copy in exchange[1:] + [(up_right, turning, handed)]:
         pl.when(receives)(copy.wait_recv)
+    landed(source, ext.at[:, 2, upper], halo_recv.at[7])
+    landed(source, ext.at[:, 2, lower], halo_recv.at[8])
+    landed(target_down, ext.at[:, 2, under_rows], halo_recv.at[9])
 
     def first(s, carry):
         forward(s, place(s), ext, probe, amps, right_fwd, left_fwd, patch, psi, far_high, far_low, sums)
@@ -316,39 +326,35 @@
     swap.wait_recv()
     got[...] += sums[mine]
 
-    scatter = []
     for k in range(1, PLANE):
         other, device = in_plane(k)
-        scatter.append(summed(k, got.at[pl.ds(other * SHARE, SHARE)], gathered.at[k - 1], device))
-        scatter[-1].start()
+        summed(1, got.at[pl.ds(other * SHARE, SHARE)], gathered.at[k - 1], device).start()
     placed(shifted, 1, place, slot_count, acc, 1)
     numer = pl.ds(0, 2)
     crossing = [(strip.at[p, lower], from_left.at[p, lower], (r, PLANE)) for p in range(2)]
     crossing += [(corner.at[p], from_corner.at[p], (r + 1, PLANE)) for p in range(2)]
-    pass_on = [remote(3 + i, src, relay, (r, spot)) for i, ((src, _, _), spot) in enumerate(zip(crossing, SUMS_RELAYS))]
-    passed = [remote(7 + i, relay, dst, device) for i, (_, dst, device) in enumerate(crossing)]
-    turned = remote(11, corner.at[numer], from_high, south)
+    pass_on = [remote(3 + i, 3, src, relay, (r, spot)) for i, ((src, _, _), spot) in enumerate(zip(crossing, SUMS_RELAYS))]
+    passed = [remote(7, 4 + i // 2, relay, dst, device) for i, (_, dst, device) in enumerate(crossing)]
+    turned = remote(8, 6, corner.at[numer], from_high, south)
     plan = [
         (turning, up_right, turned),
-        (near_right, near_left, remote(12, strip.at[numer, lower], from_left.at[numer, lower], east)),
-        (down, up, remote(13, under.at[numer], from_above.at[numer], south)),
+        (near_right, near_left, remote(9, 7, strip.at[numer, lower], from_left.at[numer, lower], east)),
+        (down, up, remote(10, 8, under.at[numer], from_above.at[numer], south)),
     ]
-    late = remote(14, strip.at[numer, upper], from_left.at[numer, upper], east)
+    late = remote(11, 9, strip.at[numer, upper], from_left.at[numer, upper], east)
     for flag, copy in zip(sourced, pass_on):
         pl.when(flag)(copy.start)
     pl.when(source)(late.start)
     for sends, _, copy in plan:
         pl.when(sends)(copy.start)
     value = got[pl.ds(xy * SHARE, SHARE)]
+    landed(None, gathered, ar_recv.at[1])
     for k in range(1, PLANE):
-        scatter[k - 1].wait_recv()
         value = value + gathered[k - 1]
     shard[...] = value
 
-    spread = []
     for k in range(1, DEPTH):
-        spread.append(summed(PLANE - 1 + k, shard, layers.at[z], in_depth(k)))
-        spread[-1].start()
+        summed(2, shard, layers.at[z], in_depth(k)).start()
     layers[z] = value
     for flag, arriving, leaving in zip(passing, pass_on, passed):
 
@@ -363,29 +369,26 @@
         strip[numer, upper] += from_high[...]
 
     pl.when(near_right)(late.start)
-    for copy in spread:
-        copy.wait_recv()
+    landed(None, layers.at[pl.ds(0, DEPTH - 1)], ar_recv.at[2])
     value = layers[0]
     for k in range(1, DEPTH):
         value = value + layers[k]
     here = pl.ds(core * HALF + xy * SHARE, SHARE)
     total[here] = value
 
-    gather = []
     for k in range(1, PLANE):
-        gather.append(summed(PLANE + DEPTH - 2 + k, total.at[here], total.at[here], in_plane(k)[1]))
-        gather[-1].start()
-
-    for copy in gather:
-        copy.wait_recv()
+        summed(3, total.at[here], total.at[here], in_plane(k)[1]).start()
+
+    others = pl.ds(core * HALF, HALF - SHARE)
+    landed(None, total.at[others], ar_recv.at[3])
     half = total.at[mine]
-    last = summed(2 * PLANE + DEPTH - 2, half, half, twin)
+    last = summed(4, half, half, twin)
     last.start()
 
     for _, receives, copy in weights + plan[1:]:
         pl.when(receives)(copy.wait_recv)
-    for flag, copy in zip([target] * 2 + [target_up] * 2, passed):
-        pl.when(flag)(copy.wait_recv)
+    landed(target, from_left.at[numer, lower], recv.at[4])
+    landed(target_up, from_corner.at[numer], recv.at[5])
     pl.when(left)(late.wait_recv)
 
     def taken(flag, value):
@@ -412,10 +415,14 @@
     scale = lax.rsqrt(total[pl.ds(8 * UNIT, UNIT)] + 1.0)
     for plane in range(8):
         direction[plane] = total[pl.ds(plane * UNIT, UNIT)] * scale
-    for copy in [swap, *scatter, *spread, *gather, last]:
+    for copy in [swap, last]:
         copy.wait_send()
-    for sends, _, copy in exchange + there + back + above + [(up_right, turning, handed)] + weights + plan:
+    landed(None, got.at[pl.ds(0, HALF - SHARE)], ar_send.at[1])
+    landed(None, layers.at[pl.ds(0, DEPTH - 1)], ar_send.at[2])
+    landed(None, total.at[others], ar_send.at[3])
+    for sends, _, copy in exchange + back + above + [(up_right, turning, handed)] + weights + plan:
         pl.when(sends)(copy.wait_send)
+    landed(target, ext.at[:, 0, pl.ds(0, 2 * W)], halo_send.at[5])
     for flag, copy in zip(sourced + passing, pass_on + passed):
         pl.when(flag)(copy.wait_send)
     pl.when(right)(late.wait_send)
@@ -432,7 +439,7 @@
     loaded = [probe, amps] + [jnp.asarray(v) for v in consts]
     slot_count, modes = amps.shape[0], probe.shape[0]
     dma = pltpu.SemaphoreType.DMA
-    messages = 2 * PLANE + DEPTH - 1
+    messages = 5
     return pl.pallas_call(
         functools.partial(step_kernel, rows, cols),
         out_shape=(
@@ -463,10 +470,10 @@
             pltpu.VMEM((W, W), F32),
             pltpu.VMEM((2, 2 * W // len(HALO_RELAYS), W), F32),
             dma((10,)),
-            dma((5 + 5 * len(HALO_RELAYS),)),
-            dma((5 + 5 * len(HALO_RELAYS),)),
-            dma((15,)),
-            dma((15,)),
+            dma((9,)),
+            dma((10,)),
+            dma((12,)),
+            dma((10,)),
             dma((messages,)),
             dma((messages,)),
             pltpu.VMEM((2, 3, 3 * W, W), F32),

time: 59.4 us -> 58 us (0.976)
  Pallas kernels: 56.4 us -> 55 us
    pallas_call x1, Pallas kernels: 56.4 us -> 55 us  [step(): pl.pallas_call(functools.partial(step_kernel, rows, cols), out_shape=(plt...]
where the time goes in v1:
time: 58 us; the launch traced here: 57.9 us
  Pallas kernels  55 us (95%)
  local copies, waits for them, and re-layouts  1.59 us (3%)
  between operations  1.29 us (2%)
    pallas_call x1, Pallas kernels, step(): pl.pallas_call(functools.partial(step_kernel, rows, cols), out_shape=(plt...  55 us
    unnamed x2, local copies, waits for them, and re-layouts  1.59 us

profile of v1, /device:TPU:1, one launch (start us, length us, event | category | flops | bytes accessed | tf_op | source)
XLA Modules:
  0.0 57.9 jit_solution(15059232682842246882)
XLA Ops:
  1.3 55.0 %step.1 = (f32[2,256,256]{2,1,0:T(8,128)S(1)}, f32[8,16,8,128]{3,2,1,0:T(8,128)S(1)}) custom-call(s32[2,8]{1,0:T(2,128)} %bitcast.5, s32[1,1]{1,0:T(1,128)} %bitcast.3.counts_hbm, f32[2,256,256]{2,1,0:T(8,128)} %refs_0_.1, f32[4,2,128,128]{3,2,1,0:T(8,128)} %refs_1_.1, f32[8,128,128]{2,1,0:T(8,128)} %refs_2_.1, bf16[768,256]{1,0:T(8,128)(2,1)} %constant.8.clone.refs_3_, ...), custom_call_target="tpu_custom_call" | custom-call | tf_op jit(solution)/shard_map/step/pallas_call | solution.py:443
  56.3 0.8 %copy.13 = f32[2,256,256]{2,1,0:T(8,128)} copy(f32[2,256,256]{2,1,0:T(8,128)S(1)} %get-tuple-element.6) | data formatting | bytes 1048576
  57.1 0.8 %copy.14 = f32[4,2,128,128]{3,2,1,0:T(8,128)} copy(f32[4,2,128,128]{3,2,1,0:T(8,128)S(1)} %bitcast.4) | data formatting | bytes 1048576

commit v2 on v1

--- a/solution.py
+++ b/solution.py
@@ -122,6 +122,11 @@
 
 
 DEPTH = 8
+PLANE_STEPS = sorted(
+    ((dx, dy) for dx in range(4) for dy in range(4) if dx + dy > 0),
+    key=lambda step: -(min(step[0], 4 - step[0]) + min(step[1], 4 - step[1])),
+)
+DEPTH_STEPS = sorted(range(1, DEPTH), key=lambda step: -min(step, DEPTH - step))
 UNIT = W // 8
 TILES = 10 * UNIT
 HALF = TILES // 2
@@ -177,11 +182,12 @@
     twin = (r + 1 - 2 * core, c)
 
     def in_plane(k):
-        other = lax.rem(xy + k, PLANE)
+        dx, dy = PLANE_STEPS[k - 1]
+        other = lax.rem(xy // 4 + dx, 4) * 4 + lax.rem(xy + dy, 4)
         return other, (r, z_hi * PLANE + other)
 
     def in_depth(k):
-        other = lax.rem(z + k, DEPTH)
+        other = lax.rem(z + DEPTH_STEPS[k - 1], DEPTH)
         half = DEPTH // 2
         return lax.rem(other, half) * 2 + core, (other // half) * PLANE + xy
 
@@ -484,8 +490,35 @@
     )(offsets.T, counts[None], obj, *loaded)
 
 
+def finish_kernel(held_object, held_direction, new_object, direction, done):
+    copies = [
+        pltpu.make_async_copy(held_object, new_object, done.at[0]),
+        pltpu.make_async_copy(held_direction, direction, done.at[1]),
+    ]
+    for copy in copies:
+        copy.start()
+    for copy in copies:
+        copy.wait()
+
+
+def finish(held_object, held_direction):
+    return pl.pallas_call(
+        finish_kernel,
+        out_shape=(
+            jax.ShapeDtypeStruct(held_object.shape, F32),
+            jax.ShapeDtypeStruct(held_direction.shape, F32),
+        ),
+        in_specs=[VMEM, VMEM],
+        out_specs=(HBM, HBM),
+        scratch_shapes=[pltpu.SemaphoreType.DMA((2,))],
+        compiler_params=pltpu.CompilerParams(vmem_limit_bytes=16 * 2**20),
+        name="finish",
+    )(held_object, held_direction)
+
+
 def body(rows, cols, object_field, probe, offsets, counts, amplitudes):
-    new_object, direction = step(object_field, probe, offsets, counts, amplitudes, rows, cols)
+    held = step(object_field, probe, offsets, counts, amplitudes, rows, cols)
+    new_object, direction = finish(*held)
     return new_object, direction.reshape(probe.shape)
 
 

time: 58 us -> 56.7 us (0.978)
  local copies, waits for them, and re-layouts: 1.59 us -> 0 us
    unnamed x2 -> x0, local copies, waits for them, and re-layouts: 1.59 us -> none
    pallas_call x0 -> x1, Pallas kernels: none -> 0.99 us  [finish(): pl.pallas_call(finish_kernel, out_shape=(jax.ShapeDtypeStruct(held_object...]
    pallas_call x1, Pallas kernels: 55 us -> 54.3 us  [step(): pl.pallas_call(functools.partial(step_kernel, rows, cols), out_shape=(plt...]
where the time goes in v2:
time: 56.7 us; the launch traced here: 56.6 us
  Pallas kernels  55.3 us (98%)
  between operations  1.29 us (2%)
    pallas_call x1, Pallas kernels, step(): pl.pallas_call(functools.partial(step_kernel, rows, cols), out_shape=(plt...  54.3 us

profile of v2, /device:TPU:1, one launch (start us, length us, event | category | flops | bytes accessed | tf_op | source)
XLA Modules:
  0.0 56.6 jit_solution(6621574923319888328)
XLA Ops:
  1.3 54.3 %step.1 = (f32[2,256,256]{2,1,0:T(8,128)S(1)}, f32[8,16,8,128]{3,2,1,0:T(8,128)S(1)}) custom-call(s32[2,8]{1,0:T(2,128)} %bitcast.4, s32[1,1]{1,0:T(1,128)} %bitcast.3.counts_hbm, f32[2,256,256]{2,1,0:T(8,128)} %refs_0_.1, f32[4,2,128,128]{3,2,1,0:T(8,128)} %refs_1_.1, f32[8,128,128]{2,1,0:T(8,128)} %refs_2_.1, bf16[768,256]{1,0:T(8,128)(2,1)} %constant.8.clone.refs_3_, ...), custom_call_target="tpu_custom_call" | custom-call | tf_op jit(solution)/shard_map/step/pallas_call | solution.py:449
  55.6 1.0 %finish.1 = (f32[2,256,256]{2,1,0:T(8,128)}, f32[8,16,8,128]{3,2,1,0:T(8,128)}) custom-call(f32[2,256,256]{2,1,0:T(8,128)S(1)} %get-tuple-element.6.held_object, f32[8,16,8,128]{3,2,1,0:T(8,128)S(1)} %get-tuple-element.7.held_direction), custom_call_target="tpu_custom_call" | custom-call | tf_op jit(solution)/shard_map/finish/pallas_call | solution.py:505

commit v3 on v2

--- a/solution.py
+++ b/solution.py
@@ -291,9 +291,6 @@
         (down, up, remote(1, 1, under.at[2], from_above.at[2], south)),
         (down_right, up_left, remote(2, 2, corner.at[2], from_corner.at[2], southeast)),
     ]
-    for sends, _, copy in weights:
-        pl.when(sends)(copy.start)
-
     for (_, flag, arriving), (_, _, leaving) in zip(there, back):
 
         @pl.when(flag)
@@ -310,6 +307,8 @@
     landed(source, ext.at[:, 2, upper], halo_recv.at[7])
     landed(source, ext.at[:, 2, lower], halo_recv.at[8])
     landed(target_down, ext.at[:, 2, under_rows], halo_recv.at[9])
+    for sends, _, copy in weights:
+        pl.when(sends)(copy.start)
 
     def first(s, carry):
         forward(s, place(s), ext, probe, amps, right_fwd, left_fwd, patch, psi, far_high, far_low, sums)

time: 56.7 us -> 56.8 us (level)
  no operation moved by 1% of the time
where the time goes in v3:
time: 56.8 us; the launch traced here: 56.7 us
  Pallas kernels  55.4 us (98%)
  between operations  1.29 us (2%)
    pallas_call x1, Pallas kernels, step(): pl.pallas_call(functools.partial(step_kernel, rows, cols), out_shape=(plt...  54.4 us

profile of v3, /device:TPU:1, one launch (start us, length us, event | category | flops | bytes accessed | tf_op | source)
XLA Modules:
  0.0 56.7 jit_solution(18227168971218719626)
XLA Ops:
  1.3 54.4 %step.1 = (f32[2,256,256]{2,1,0:T(8,128)S(1)}, f32[8,16,8,128]{3,2,1,0:T(8,128)S(1)}) custom-call(s32[2,8]{1,0:T(2,128)} %bitcast.4, s32[1,1]{1,0:T(1,128)} %bitcast.3.counts_hbm, f32[2,256,256]{2,1,0:T(8,128)} %refs_0_.1, f32[4,2,128,128]{3,2,1,0:T(8,128)} %refs_1_.1, f32[8,128,128]{2,1,0:T(8,128)} %refs_2_.1, bf16[768,256]{1,0:T(8,128)(2,1)} %constant.8.clone.refs_3_, ...), custom_call_target="tpu_custom_call" | custom-call | tf_op jit(solution)/shard_map/step/pallas_call | solution.py:448
  55.7 1.0 %finish.1 = (f32[2,256,256]{2,1,0:T(8,128)}, f32[8,16,8,128]{3,2,1,0:T(8,128)}) custom-call(f32[2,256,256]{2,1,0:T(8,128)S(1)} %get-tuple-element.6.held_object, f32[8,16,8,128]{3,2,1,0:T(8,128)S(1)} %get-tuple-element.7.held_direction), custom_call_target="tpu_custom_call" | custom-call | tf_op jit(solution)/shard_map/finish/pallas_call | solution.py:504

commit v4 on v2

--- a/solution.py
+++ b/solution.py
@@ -205,6 +205,15 @@
     target_down = jnp.logical_and(source, down)
     greetings = [(source, (r, PLANE + spot)) for spot in HALO_RELAYS]
     greetings += [(target_down, (r + 1, PLANE + spot)) for spot in HALO_RELAYS]
+    for when, device in greetings:
+
+        @pl.when(when)
+        def _():
+            pl.semaphore_signal(barrier, inc=1, device_id=device, device_id_type=MESH)
+
+    for device in peers:
+        pl.semaphore_signal(barrier, inc=1, device_id=device, device_id_type=MESH)
+    greetings = []
     greetings += [(flag, (r, PLANE)) for flag in ahead] + [(near_right, east), (down, south)]
     waits = [near_left, up, *[target for _ in HALO_RELAYS], *ahead, *ahead_up]
     greetings += [(left, (r, c - 1)), (up, (r - 1, c)), (up_left, (r - 1, c - 1))]
@@ -217,8 +226,6 @@
         def _():
             pl.semaphore_signal(barrier, inc=1, device_id=device, device_id_type=MESH)
 
-    for device in peers:
-        pl.semaphore_signal(barrier, inc=1, device_id=device, device_id_type=MESH)
     waits += [right, down, down_right, *sourced, *passing]
 
     def place(s):
@@ -269,6 +276,15 @@
     pl.semaphore_wait(barrier, len(peers) + count(*waits))
     for sends, _, copy in there + exchange:
         pl.when(sends)(copy.start)
+    for (_, flag, arriving), (_, _, leaving) in zip(there, back):
+
+        @pl.when(flag)
+        def _():
+            arriving.wait_recv()
+            leaving.start()
+
+    for flag, _, copy in above:
+        pl.when(flag)(copy.start)
 
     shifted[...] = jnp.zeros_like(shifted)
     sums[...] = jnp.zeros_like(sums)
@@ -294,15 +310,6 @@
     for sends, _, copy in weights:
         pl.when(sends)(copy.start)
 
-    for (_, flag, arriving), (_, _, leaving) in zip(there, back):
-
-        @pl.when(flag)
-        def _():
-            arriving.wait_recv()
-            leaving.start()
-
-    for flag, _, copy in above:
-        pl.when(flag)(copy.start)
     pl.when(near_right)(exchange[0][2].wait_recv)
     pl.when(up_right)(handed.start)
     for _, receives, copy in exchange[1:] + [(up_right, turning, handed)]:

time: 56.7 us -> 56.7 us (level)
  no operation moved by 1% of the time
where the time goes in v4:
time: 56.7 us; the launch traced here: 56.6 us
  Pallas kernels  55.3 us (98%)
  between operations  1.29 us (2%)
    pallas_call x1, Pallas kernels, step(): pl.pallas_call(functools.partial(step_kernel, rows, cols), out_shape=(plt...  54.3 us

profile of v4, /device:TPU:1, one launch (start us, length us, event | category | flops | bytes accessed | tf_op | source)
XLA Modules:
  0.0 56.6 jit_solution(8975653389766046677)
XLA Ops:
  1.3 54.3 %step.1 = (f32[2,256,256]{2,1,0:T(8,128)S(1)}, f32[8,16,8,128]{3,2,1,0:T(8,128)S(1)}) custom-call(s32[2,8]{1,0:T(2,128)} %bitcast.4, s32[1,1]{1,0:T(1,128)} %bitcast.3.counts_hbm, f32[2,256,256]{2,1,0:T(8,128)} %refs_0_.1, f32[4,2,128,128]{3,2,1,0:T(8,128)} %refs_1_.1, f32[8,128,128]{2,1,0:T(8,128)} %refs_2_.1, bf16[768,256]{1,0:T(8,128)(2,1)} %constant.8.clone.refs_3_, ...), custom_call_target="tpu_custom_call" | custom-call | tf_op jit(solution)/shard_map/step/pallas_call | solution.py:456
  55.6 1.0 %finish.1 = (f32[2,256,256]{2,1,0:T(8,128)}, f32[8,16,8,128]{3,2,1,0:T(8,128)}) custom-call(f32[2,256,256]{2,1,0:T(8,128)S(1)} %get-tuple-element.6.held_object, f32[8,16,8,128]{3,2,1,0:T(8,128)S(1)} %get-tuple-element.7.held_direction), custom_call_target="tpu_custom_call" | custom-call | tf_op jit(solution)/shard_map/finish/pallas_call | solution.py:512

commit v5 on v2

--- a/solution.py
+++ b/solution.py
@@ -90,7 +90,7 @@
 
     ore, oim = cut(0), cut(1)
     patch[s, 0], patch[s, 1] = ore, oim
-    add_plane(sums, 8, ore * ore + oim * oim)
+    add_plane(sums, WEIGHT, ore * ore + oim * oim)
     inten = jnp.zeros((W, W), F32)
     far = []
     for g in range(0, probe.shape[0], 2):
@@ -107,17 +107,16 @@
         far_high[s, m], far_low[s, m] = hilo(columns([real * factor, imag * factor]))
 
 
-def backward(s, probe, table_right, table_left, patch, psi, far_high, far_low, sums):
+def backward(s, g, probe, table_right, table_left, patch, psi, far_high, far_low, sums):
     num_re, num_im = jnp.zeros((W, W), F32), jnp.zeros((W, W), F32)
-    for g in range(0, probe.shape[0], 2):
-        high, low = rows_of([far_high[s, g], far_high[s, g + 1]]), rows_of([far_low[s, g], far_low[s, g + 1]])
-        pairs = times_left(times_right(high, low, table_right), table_left)
-        for m, (real, imag) in zip((g, g + 1), pairs):
-            chi_re, chi_im = real - psi[s, m, 0], imag - psi[s, m, 1]
-            num_re = num_re + (probe[m, 0] * chi_re + probe[m, 1] * chi_im)
-            num_im = num_im + (probe[m, 0] * chi_im - probe[m, 1] * chi_re)
-            add_plane(sums, 2 * m, patch[s, 0] * chi_re + patch[s, 1] * chi_im)
-            add_plane(sums, 2 * m + 1, patch[s, 0] * chi_im - patch[s, 1] * chi_re)
+    high, low = rows_of([far_high[s, g], far_high[s, g + 1]]), rows_of([far_low[s, g], far_low[s, g + 1]])
+    pairs = times_left(times_right(high, low, table_right), table_left)
+    for m, (real, imag) in zip((g, g + 1), pairs):
+        chi_re, chi_im = real - psi[s, m, 0], imag - psi[s, m, 1]
+        num_re = num_re + (probe[m, 0] * chi_re + probe[m, 1] * chi_im)
+        num_im = num_im + (probe[m, 0] * chi_im - probe[m, 1] * chi_re)
+        add_plane(sums, MODE_PLANES[2 * m], patch[s, 0] * chi_re + patch[s, 1] * chi_im)
+        add_plane(sums, MODE_PLANES[2 * m + 1], patch[s, 0] * chi_im - patch[s, 1] * chi_re)
     return num_re, num_im
 
 
@@ -131,6 +130,7 @@
 TILES = 10 * UNIT
 HALF = TILES // 2
 SHARE = HALF // PLANE
+MODE_PLANES, WEIGHT = (0, 1, 2, 3, 5, 6, 7, 8), 4
 
 
 def add_plane(sums, plane, value):
@@ -317,17 +317,20 @@
 
     lax.fori_loop(0, slot_count, first, 0, unroll=True)
 
-    def second(s, carry):
+    def second(g, s, carry):
         turn = place(s)[1] % W
-        for plane, value in enumerate(backward(s, probe, right_inv, left_inv, patch, psi, far_high, far_low, sums)):
-            shifted[s, plane, pl.ds(2 * W, W), :] = pltpu.roll(value, turn, 1)
+        here = pl.ds(2 * W, W)
+        for plane, value in enumerate(backward(s, g, probe, right_inv, left_inv, patch, psi, far_high, far_low, sums)):
+            value = pltpu.roll(value, turn, 1)
+            shifted[s, plane, here, :] = value if g == 0 else shifted[s, plane, here, :] + value
         return carry
-
-    lax.fori_loop(0, slot_count, second, 0, unroll=True)
 
     mine = pl.ds(core * HALF, HALF)
     swap = summed(0, sums.at[pl.ds((1 - core) * HALF, HALF)], got, twin)
-    swap.start()
+    lax.fori_loop(0, slot_count, functools.partial(second, 0), 0, unroll=True)
+    pl.when(core == 1)(swap.start)
+    lax.fori_loop(0, slot_count, functools.partial(second, 2), 0, unroll=True)
+    pl.when(core == 0)(swap.start)
     placed(shifted, 0, place, slot_count, acc, 0)
     swap.wait_recv()
     got[...] += sums[mine]
@@ -418,9 +421,9 @@
                 updated[plane, span, pl.ds(j * W, W)] = ext[plane, j, span, :] + parts[plane] * scale
 
     last.wait_recv()
-    scale = lax.rsqrt(total[pl.ds(8 * UNIT, UNIT)] + 1.0)
-    for plane in range(8):
-        direction[plane] = total[pl.ds(plane * UNIT, UNIT)] * scale
+    scale = lax.rsqrt(total[pl.ds(WEIGHT * UNIT, UNIT)] + 1.0)
+    for k, plane in enumerate(MODE_PLANES):
+        direction[k] = total[pl.ds(plane * UNIT, UNIT)] * scale
     for copy in [swap, last]:
         copy.wait_send()
     landed(None, got.at[pl.ds(0, HALF - SHARE)], ar_send.at[1])

time: 56.7 us -> 57.6 us (1.016)
  Pallas kernels: 55.3 us -> 56.2 us
    pallas_call x1, Pallas kernels: 54.3 us -> 55.2 us  [step(): pl.pallas_call(functools.partial(step_kernel, rows, cols), out_shape=(plt...]
where the time goes in v5:
time: 57.6 us; the launch traced here: 57.5 us
  Pallas kernels  56.2 us (98%)
  between operations  1.29 us (2%)
    pallas_call x1, Pallas kernels, step(): pl.pallas_call(functools.partial(step_kernel, rows, cols), out_shape=(plt...  55.2 us

profile of v5, /device:TPU:1, one launch (start us, length us, event | category | flops | bytes accessed | tf_op | source)
XLA Modules:
  0.0 57.5 jit_solution(5458628941618420234)
XLA Ops:
  1.3 55.2 %step.1 = (f32[2,256,256]{2,1,0:T(8,128)S(1)}, f32[8,16,8,128]{3,2,1,0:T(8,128)S(1)}) custom-call(s32[2,8]{1,0:T(2,128)} %bitcast.4, s32[1,1]{1,0:T(1,128)} %bitcast.3.counts_hbm, f32[2,256,256]{2,1,0:T(8,128)} %refs_0_.1, f32[4,2,128,128]{3,2,1,0:T(8,128)} %refs_1_.1, f32[8,128,128]{2,1,0:T(8,128)} %refs_2_.1, bf16[768,256]{1,0:T(8,128)(2,1)} %constant.8.clone.refs_3_, ...), custom_call_target="tpu_custom_call" | custom-call | tf_op jit(solution)/shard_map/step/pallas_call | solution.py:452
  56.5 1.0 %finish.1 = (f32[2,256,256]{2,1,0:T(8,128)}, f32[8,16,8,128]{3,2,1,0:T(8,128)}) custom-call(f32[2,256,256]{2,1,0:T(8,128)S(1)} %get-tuple-element.6.held_object, f32[8,16,8,128]{3,2,1,0:T(8,128)S(1)} %get-tuple-element.7.held_direction), custom_call_target="tpu_custom_call" | custom-call | tf_op jit(solution)/shard_map/finish/pallas_call | solution.py:508
